TPU v7x, 128 devices: a whole 4x4x4 slice. The times are simulated.
128 devices in a mesh: item: 64 (over z, y, x_hi, core), qgrp: 2 (over x_lo).
Axes of the slice: x: 4 (x_hi: 2, x_lo: 2; x = x_hi * 2 + x_lo), y: 4, z: 4, core: 2. Of those that a mesh axis runs over, the one named last changes fastest.
Arguments:
- hidden: bfloat16 [131072, 3584], P(('item', 'qgrp')), may hold values from -6 to 6
- w_query: bfloat16 [3584, 1024], P(('item', 'qgrp')), may hold values from -0.09375 to 0.09375
- adapter: bfloat16 [1024, 1024], replicated, may hold values from -0.1875 to 0.1875
- item_emb: bfloat16 [2048, 1024], P(('item', 'qgrp')), may hold values from -120 to 120
- counts: int32 [2048], replicated, may hold values from 256 to 4095
- positive: int32 [131072], P(('item', 'qgrp')), may hold values from 0 to 2047
- loss_weight: float32 [131072], P(('item', 'qgrp')), may hold values from 0.02 to 0.1
Outputs:
- grad_query_weight: float32 [3584, 1024], P(('item', 'qgrp'))
- grad_adapter: float32 [1024, 1024], P(('item', 'qgrp'))
- loss: float32 [], replicated
All inputs are finite; a program needn't handle non-finite values.
Results may differ from a plain program's by a relative error of at most 0.0047.
Values may be sent and summed in bfloat16 or wider, within the bound.
A program may use at most 128 MiB of HBM per device.

v0:
```python
import math

import jax
import jax.numpy as jnp
from jax import lax
from jax.sharding import PartitionSpec as P


def on_device(hidden, w_query, adapter, item_emb, counts, positive, loss_weight):
    scale = 2.0 / math.sqrt(adapter.shape[0])
    query_rows = hidden.shape[0]
    devices_all = lax.axis_size(("item", "qgrp"))
    whole_weight = lax.all_gather(w_query, ("item", "qgrp"), axis=0, tiled=True)
    queries = jnp.dot(hidden, whole_weight, preferred_element_type=jnp.float32).astype(jnp.bfloat16)
    log_count = jnp.log(counts.astype(jnp.float32))
    owned = (
        item_emb.astype(jnp.float32)
        + jnp.dot(item_emb, adapter, preferred_element_type=jnp.float32)
    ).astype(jnp.bfloat16)
    adapted = lax.all_gather(owned, ("item", "qgrp"), axis=0, tiled=True)
    pool_size = adapted.shape[0]
    logits = (
        scale * jnp.dot(queries, adapted.T, preferred_element_type=jnp.float32) - log_count[None, :]
    )
    top = jnp.max(logits, axis=1, keepdims=True)
    shifted = jnp.exp(logits - top)
    denom = jnp.sum(shifted, axis=1, keepdims=True)
    onehot = (jnp.arange(pool_size, dtype=jnp.int32)[None, :] == positive[:, None]).astype(
        jnp.float32
    )
    picked = jnp.sum(logits * onehot, axis=1)
    losses = jnp.log(denom[:, 0]) + top[:, 0] - picked
    coeff = (loss_weight[:, None] * (shifted / denom - onehot)).astype(jnp.bfloat16)
    grad_q = (scale * jnp.dot(coeff, adapted, preferred_element_type=jnp.float32)).astype(
        jnp.bfloat16
    )
    grad_query_weight = lax.psum_scatter(
        jnp.einsum("qh,qe->he", hidden, grad_q, preferred_element_type=jnp.float32),
        ("item", "qgrp"),
        scatter_dimension=0,
        tiled=True,
    )
    own_grad = lax.psum_scatter(
        scale * jnp.einsum("qn,qe->ne", coeff, queries, preferred_element_type=jnp.float32),
        ("item", "qgrp"),
        scatter_dimension=0,
        tiled=True,
    )
    partial_adapter = jnp.einsum(
        "na,nb->ab", item_emb.astype(jnp.float32), own_grad, precision=lax.Precision.HIGHEST
    )
    grad_adapter = lax.psum_scatter(
        partial_adapter, ("item", "qgrp"), scatter_dimension=0, tiled=True
    )
    total = lax.psum(jnp.sum(loss_weight * losses), ("item", "qgrp"))
    loss = total / (query_rows * devices_all)
    return (grad_query_weight, grad_adapter, loss)


def solution(mesh):
    placed = (
        P(("item", "qgrp"), None),
        P(("item", "qgrp"), None),
        P(),
        P(("item", "qgrp"), None),
        P(),
        P(("item", "qgrp")),
        P(("item", "qgrp")),
    )
    return jax.shard_map(
        on_device,
        mesh=mesh,
        in_specs=placed,
        out_specs=(P(("item", "qgrp"), None), P(("item", "qgrp"), None), P()),
        check_vma=False,
    )
```

profile of v0, /device:TPU:1, one launch (start us, length us, event | category | flops | bytes accessed | tf_op | source)
XLA Modules:
  0.0 2128.1 jit_solution(637103023729611184)
XLA Ops:
  7.2 0.0 copy-start
  7.2 0.0 all-gather.6.cloned.1.call-start
  7.2 0.7 all-gather.6.cloned.1.call-update
  7.9 0.0 all-gather.4.cloned.1.call-start
  8.0 0.8 copy-done
  8.8 1.8 fusion.3
  10.6 0.0 all-gather.4.cloned.1.call-update
  10.6 0.0 reduce-scatter.6.cloned.1.call-start
  10.7 0.7 convert_log_fusion
  11.4 314.3 %all-gather.6.cloned.1.call-done = bf16[128,28,1024]{2,1,0:T(8,128)(2,1)} async-done(((bf16[1,28,1024]{2,1,0:T(8,128)(2,1)}), bf16[128,28,1024]{2,1,0:T(8,128)(2,1)}) %all-gather.6.cloned.1.call-update) | async-done | bytes 7340048 | tf_op jit(solution)/shard_map/all_gather | solution.py:13
  325.7 10.9 reshape.12
  336.7 13.2 convolution_convert_fusion
  349.8 285.0 %all-gather.4.cloned.1.call-done = bf16[2048,1024]{1,0:T(8,128)(2,1)} async-done(((bf16[16,1024]{1,0:T(8,128)(2,1)}), bf16[2048,1024]{1,0:T(8,128)(2,1)}) %all-gather.4.cloned.1.call-update) | async-done | bytes 4194320 | tf_op jit(solution)/shard_map/all_gather | solution.py:20
  634.8 7.2 fusion.1
  642.0 0.0 copy-start.6
  642.0 4.2 select_reduce_fusion
  646.2 10.1 convolution_multiply_fusion
  656.3 0.0 reduce-scatter.6.cloned.1.call-update
  656.4 0.2 all-reduce.3.cloned.1.call-start
  656.6 25.2 %convolution_bitcast_fusion = f32[3584,1024]{0,1:T(8,128)} fusion(bf16[1024,3584]{1,0:T(8,128)(2,1)} %param.7, bf16[2048,1024]{1,0:T(8,128)(2,1)} %all-gather.4.cloned.1.call-done, f32[1024,2048]{1,0:T(8,128)} %copy-done.2, s32[1024]{0:T(1024)S(1)} %copy-done.5, f32[1024]{0:T(1024)S(1)} %get-tuple-element.13, f32[1024]{0:T(1024)S(1)} %get-tuple-element.14, ...), kind=kOutput, calls=%fused_computation | convolution fusion | flops 11832131584 | bytes 34627584 | tf_op jit(solution)/shard_map/qh,qe->he/dot_general | solution.py:38
  681.8 0.0 all-reduce.3.cloned.1.call-update
  681.8 0.3 reduce-scatter.8.cloned.1.call-start
  682.1 621.1 %reduce-scatter.6.cloned.1.call-done = f32[16,1024]{1,0:T(8,128)} async-done(((f32[2048,1024]{1,0:T(8,128)}), f32[16,1024]{1,0:T(8,128)}) %reduce-scatter.6.cloned.1.call-update) | async-done | bytes 65552 | tf_op jit(solution)/shard_map/reduce_scatter | solution.py:43
  1303.2 4.7 convolution_bitcast_fusion.1
  1307.9 5.4 copy.18
  1313.3 0.0 reduce-scatter.8.cloned.1.call-update
  1313.3 0.6 multiply_reduce_fusion
  1313.9 67.4 %psum.7 = f32[]{:T(128)} all-reduce(f32[]{:T(128)} %multiply_reduce_fusion), channel_id=1, replica_groups=mesh['item'=64,'qgrp'=2] {'item','qgrp'}, use_global_device_ids=true, to_apply=%region_7.0 | all-reduce | flops 1 | bytes 8 | tf_op jit(solution)/shard_map/psum | solution.py:55
  1382.0 99.3 %all-reduce.3.cloned.1.call-done = f32[3584,1024]{0,1:T(8,128)} async-done(((f32[3584,1024]{0,1:T(8,128)}), f32[3584,1024]{0,1:T(8,128)}) %all-reduce.3.cloned.1.call-update) | async-done | bytes 14680080
  1481.2 1.4 constant_dynamic-slice_fusion
  1482.6 0.9 copy.14
  1483.5 636.9 %reduce-scatter.8.cloned.1.call-done = f32[8,1024]{1,0:T(8,128)} async-done(((f32[1024,1024]{1,0:T(8,128)}), f32[8,1024]{1,0:T(8,128)}) %reduce-scatter.8.cloned.1.call-update) | async-done | bytes 32784
  (13 shorter events, 0.0 us)
Async XLA Ops:
  7.2 1.6 copy-start
  7.2 318.5 %all-gather.6.cloned.1.call-start = ((), (), s32[]{:S(2)}) async-start(), calls=%async_computation.4 | async-start | bytes 8454144 | tf_op jit(solution)/shard_map/all_gather | solution.py:13
  7.9 626.9 %all-gather.4.cloned.1.call-start = ((), (), s32[]{:S(2)}) async-start(), calls=%async_computation.2 | async-start | bytes 4227072 | tf_op jit(solution)/shard_map/all_gather | solution.py:20
  10.6 1292.6 %reduce-scatter.6.cloned.1.call-start = ((), (), s32[]{:S(2)}) async-start(), calls=%async_computation.3 | async-start | bytes 8454144 | tf_op jit(solution)/shard_map/reduce_scatter | solution.py:43
  349.8 292.2 %copy-start.5 = (s32[1024]{0:T(1024)S(1)}, s32[1024]{0:T(1024)}, u32[]{:S(2)}) copy-start(s32[1024]{0:T(1024)} %param.12) | copy-start | bytes 12292
  642.0 4.2 copy-start.2
  642.0 4.2 copy-start.6
  642.0 4.2 copy-start.7
  656.4 824.9 %all-reduce.3.cloned.1.call-start = ((), (), s32[]{:S(2)}) async-start(), calls=%async_computation.6 | async-start | bytes 29360128
  681.8 621.4 %copy-start.3 = (bf16[16,1024]{1,0:T(8,128)(2,1)S(1)}, bf16[16,1024]{1,0:T(8,128)(2,1)}, u32[]{:S(2)}) copy-start(bf16[16,1024]{1,0:T(8,128)(2,1)} %param.10) | copy-start | bytes 98308
  681.8 631.5 %copy-start.4 = (f32[1024]{0:T(1024)S(1)}, f32[1024]{0:T(1024)}, u32[]{:S(2)}) copy-start(f32[1024]{0:T(1024)} %get-tuple-element.12) | copy-start | bytes 12292
  681.8 1438.6 %copy-start.1 = (bf16[1024,1024]{1,0:T(8,128)(2,1)S(1)}, bf16[1024,1024]{1,0:T(8,128)(2,1)}, u32[]{:S(2)}) copy-start(bf16[1024,1024]{1,0:T(8,128)(2,1)} %param.9) | copy-start | bytes 6291460
  681.8 1438.6 %reduce-scatter.8.cloned.1.call-start = ((), (), s32[]{:S(2)}) async-start(), calls=%async_computation.5 | async-start | bytes 4227072
Sparse Core Ops, SparseCore 0:
  9.7 315.9 all-gather.5
  328.0 306.7 all-gather.3
  656.5 646.6 reduce-scatter.5
  1308.9 172.2 all-reduce.2
  1484.0 636.3 reduce-scatter.7
where the time goes:
time: 2130 us
  waiting for transfers between devices  1960 us (92%)
  blocking collectives  67.4 us (3%)
  matrix products  62.2 us (3%)
    unnamed x7, waiting for transfers between devices  737 us
    reduce_scatter x1, waiting for transfers between devices, on_device(): lax.psum_scatter(scale * jnp.einsum('qn,qe->ne', coeff, queries, preferre...  621 us
    all_gather x1, waiting for transfers between devices, on_device(): whole_weight = lax.all_gather(w_query, ('item', 'qgrp'), axis=0, tiled=True)  314 us
    all_gather x1, waiting for transfers between devices, on_device(): adapted = lax.all_gather(owned, ('item', 'qgrp'), axis=0, tiled=True)  285 us
    psum x1, blocking collectives, on_device(): total = lax.psum(jnp.sum(loss_weight * losses), ('item', 'qgrp'))  67.4 us
  transfers between devices with their start and end apart: 5, of which 5 were waited for; matrix products, arithmetic and copies ran while one was open for 3% of the time, Pallas kernels for 0%

commit v1 on v0

v1 whole, which is shorter than its diff:
```python
import functools
import math

import jax
import jax.numpy as jnp
from jax import lax
from jax.experimental import pallas as pl
from jax.experimental.pallas import tpu as pltpu
from jax.sharding import PartitionSpec as P

MESH = pl.DeviceIdType.MESH
F32, BF16 = jnp.float32, jnp.bfloat16
AXES = ("item", "qgrp")
LINE = 8
SIDE = 4
QUARTERS, WIDE = 4, 256
ROWS = 256


def dot(a, b, contract=(1, 0)):
    dims = (((contract[0],), (contract[1],)), ((), ()))
    return lax.dot_general(a, b, dims, preferred_element_type=F32)


def place():
    item, low = lax.axis_index("item"), lax.axis_index("qgrp")
    return item // 16, (item // 4) % 4, (item // 2) % 2, item % 2, low


def device(z, y, high, core, low):
    return (z * 16 + y * 4 + high * 2 + core, low)


def select(shape, source):
    row = lax.broadcasted_iota(jnp.int32, shape, 0)
    col = lax.broadcasted_iota(jnp.int32, shape, 1)
    return jnp.where(col == source(row), 1.0, 0.0).astype(BF16)


def step_kernel(
    scale, hidden_ref, w_ref, adapter_ref, item_ref, counts_ref, positive_ref, weight_ref,
    gw_ref, ga_ref, loss_ref,
    hid, hid_t, ada, wall, xs, pool, adapted, queries, grad_q, pulled, pos_col, weight_col, log_count,
    sib_in, first_z, first_y, second_in, slot_out, slot_in, loss_out, loss_in,
    load_sem, xs_s, xs_r, w_s, w_r, ws_s, ws_r, e_s, e_r, sib_s, sib_r, fz_s, fz_r, fy_s, fy_r, se_s, se_r,
    sl_s, sl_r, lo_s, lo_r,
):
    z, y, high, core, low = place()
    slot = high * 4 + core * 2 + low
    block_rows = LINE * w_ref.shape[0]
    own_rows = w_ref.shape[0]
    adapter_rows = ga_ref.shape[0]
    group = SIDE * block_rows
    sibling = device(z, y, high, 1 - core, low)

    def z_peer(o):
        return device((z + o) % SIDE, y, high, core, low)

    def y_peer(o):
        return device(z, (y + o) % SIDE, high, core, low)

    def flip(k):
        return (high + k // 4) % 2, (core + (k // 2) % 2) % 2, (low + k % 2) % 2

    def line_peer(k):
        h, c, l = flip(k)
        return device(z, y, h, c, l)

    def line_slot(k):
        h, c, l = flip(k)
        return h * 4 + c * 2 + l

    def remote(src, dst, send, recv, to):
        return pltpu.make_async_remote_copy(
            src_ref=src, dst_ref=dst, send_sem=send, recv_sem=recv, device_id=to, device_id_type=MESH
        )

    loads = [
        pltpu.make_async_copy(hidden_ref.at[:, pl.ds(group * k, group)], hid.at[k], load_sem.at[k])
        for k in range(SIDE)
    ]
    loads.append(pltpu.make_async_copy(adapter_ref, ada, load_sem.at[SIDE]))
    for load in loads:
        load.start()

    barrier = pltpu.get_barrier_semaphore()
    peers = [line_peer(k) for k in range(1, LINE)]
    peers += [z_peer(o) for o in (1, 2, 3)] + [y_peer(o) for o in (1, 2, 3)]
    for peer in peers:
        pl.semaphore_signal(barrier, inc=1, device_id=peer, device_id_type=MESH)

    xs[slot, :, own_rows:, :] = jnp.zeros((QUARTERS, 32 - own_rows, WIDE), BF16)
    for q in range(QUARTERS):
        xs[slot, q, 0:own_rows, :] = w_ref[:, q * WIDE:(q + 1) * WIDE]
    pool[z, y, slot] = item_ref[...]
    pl.semaphore_wait(barrier, len(peers))

    sent = []

    def send(copy):
        copy.start()
        sent.append(copy)

    for k in (2, 1, 3, 4, 6, 5, 7):
        pair = pl.ds(2 * flip(k)[1], 2)
        send(remote(xs.at[slot, pair], xs.at[slot, pair], xs_s.at[k], xs_r.at[k], line_peer(k)))
    own_e = pool.at[z, y, slot]
    for o in (1, 2, 3):
        send(remote(own_e, own_e, e_s.at[o - 1], e_r.at[o - 1], z_peer(o)))

    log_count[...] = jnp.log(counts_ref[...].astype(F32))
    for r in range(positive_ref.shape[0]):
        rows = pl.ds(r * 128, 128)
        line = positive_ref[r:r + 1, :].astype(F32)
        pos_col[rows, :] = jnp.broadcast_to(line, (128, 128)).T
        weight_col[rows, :] = jnp.broadcast_to(weight_ref[r:r + 1, :], (128, 128)).T

    for o in (1, 2, 3):
        got = pool.at[(z - o + SIDE) % SIDE, y, slot]
        remote(got, got, e_s.at[o - 1], e_r.at[o - 1], z_peer(o)).wait_recv()
    column_e = pool.at[:, y, slot]
    for o in (1, 2, 3):
        send(remote(column_e, column_e, e_s.at[2 + o], e_r.at[2 + o], y_peer(o)))

    for k in range(1, LINE):
        got = xs.at[line_slot(k), pl.ds(2 * core, 2)]
        remote(got, got, xs_s.at[k], xs_r.at[k], line_peer(k)).wait_recv()
    half = 4 * own_rows

    def source(row):
        skipped = sum(jnp.where(row >= own_rows * s, 32 - own_rows, 0) for s in (1, 2, 3))
        return row + skipped

    pick = select((half, 128), source)
    here = z * SIDE + y
    for p in range(2):
        q = 2 * core + p
        for h in range(2):
            padded = jnp.reshape(xs[4 * h:4 * h + 4, q], (128, WIDE))
            wall[q, here, half * h:half * (h + 1), :] = dot(pick, padded).astype(BF16)

    def w_block(p, of, og):
        if p == 0:
            b = ((z - og + SIDE) % SIDE) * SIDE + (y - of + SIDE) % SIDE
        else:
            b = ((z - of + SIDE) % SIDE) * SIDE + (y - og + SIDE) % SIDE
        return b

    def w_at(p, of, og, c=None):
        q = 2 * (core if c is None else c) + p
        return wall.at[q, w_block(p, of, og), pl.ds(0, block_rows)]

    def w_send(p, of, og, new_of, new_og, to):
        at = w_at(p, of, og)
        n = new_of * SIDE + new_og
        send(remote(at, at, w_s.at[p, n], w_r.at[p, n], to))

    def w_wait(p, of, og):
        at = w_at(p, of, og)
        n = of * SIDE + og
        remote(at, at, w_s.at[p, n], w_r.at[p, n], sibling).wait_recv()

    def w_share(p, of, og):
        at = w_at(p, of, og)
        n = of * SIDE + og
        send(remote(at, at, ws_s.at[p, n], ws_r.at[p, n], sibling))

    near = ((y_peer, z_peer), (z_peer, y_peer))
    for o in (1, 3, 2):
        for p in range(2):
            w_send(p, 0, 0, o, 0, near[p][0](o))
    for o in (1, 3, 2):
        for p in range(2):
            w_send(p, 0, 0, 0, o, near[p][1](o))
    for p in range(2):
        w_share(p, 0, 0)

    for o in (1, 2, 3):
        got = pool.at[:, (y - o + SIDE) % SIDE, slot]
        remote(got, got, e_s.at[2 + o], e_r.at[2 + o], y_peer(o)).wait_recv()
    slab = pool.at[:, :, slot]
    for n, k in enumerate((1, 4, 5)):
        send(remote(slab, slab, e_s.at[6 + n], e_r.at[6 + n], line_peer(k)))
    send(remote(slab, slab, e_s.at[9], e_r.at[9], sibling))

    for of in (1, 3, 2):
        for p in range(2):
            w_wait(p, of, 0)
            for og in (1, 3, 2):
                w_send(p, of, 0, of, og, near[p][1](og))
            w_share(p, of, 0)

    for k in range(SIDE):
        loads[k].wait()
        for s in range(group // 128):
            hid_t[k, 128 * s:128 * (s + 1), :] = hid[k, :, 128 * s:128 * (s + 1)].T
        if k == 1:
            for p in range(2):
                for og in (1, 3, 2):
                    w_wait(p, 0, og)
                    w_share(p, 0, og)
    for n, k in enumerate((1, 4, 5)):
        got = pool.at[:, :, line_slot(k)]
        remote(got, got, e_s.at[6 + n], e_r.at[6 + n], line_peer(k)).wait_recv()
        send(remote(got, got, e_s.at[10 + n], e_r.at[10 + n], sibling))
    for p in range(2):
        for of in (1, 3, 2):
            for og in (1, 3, 2):
                w_wait(p, of, og)
                w_share(p, of, og)
    for n, k in enumerate((2, 3, 6, 7)):
        got = pool.at[:, :, line_slot(k)]
        remote(got, got, e_s.at[9 + n], e_r.at[9 + n], sibling).wait_recv()

    loads[SIDE].wait()
    chunk = pool.shape[2] * pool.shape[3] * 2

    def adapt(i, carry):
        rows = pl.ds(pl.multiple_of(i * chunk, chunk), chunk)
        items = jnp.reshape(pool[i // 2, pl.ds((i % 2) * 2, 2)], (chunk, pool.shape[4]))
        adapted[rows, :] = (items.astype(F32) + dot(items, ada[...])).astype(BF16)
        return carry

    lax.fori_loop(0, adapted.shape[0] // chunk, adapt, 0)

    for p in range(2):
        for of in range(SIDE):
            for og in range(SIDE):
                at = w_at(p, of, og, 1 - core)
                n = of * SIDE + og
                remote(at, at, ws_s.at[p, n], ws_r.at[p, n], sibling).wait_recv()

    def project(i, carry):
        cols = pl.ds(pl.multiple_of(i * WIDE, WIDE), WIDE)
        total = None
        for k in range(SIDE):
            part = jnp.reshape(wall[i, SIDE * k:SIDE * (k + 1), 0:block_rows, :], (group, WIDE))
            term = dot(hid[k], part)
            total = term if total is None else total + term
        queries[:, cols] = total.astype(BF16)
        return carry

    lax.fori_loop(0, QUARTERS, project, 0)

    items_all = adapted.shape[0]

    def softmax(i, total):
        rows = pl.ds(pl.multiple_of(i * ROWS, ROWS), ROWS)
        logits = scale * dot(queries[rows, :], adapted[...], (1, 1)) - log_count[...]
        top = jnp.max(logits, axis=1, keepdims=True)
        shifted = jnp.exp(logits - top)
        denom = jnp.sum(shifted, axis=1, keepdims=True)
        lane = lax.broadcasted_iota(jnp.int32, (ROWS, items_all), 1).astype(F32)
        hit = lane == pos_col[rows, 0:1]
        picked = jnp.sum(jnp.where(hit, logits, 0.0), axis=1, keepdims=True)
        weight = weight_col[rows, 0:1]
        losses = jnp.log(denom) + top - picked
        plain = shifted * (weight / denom)
        coeff = jnp.where(hit, plain - weight, plain).astype(BF16)
        grad_q[rows, :] = (scale * dot(coeff, adapted[...])).astype(BF16)
        items = jnp.reshape(pool[...], (items_all, pool.shape[4]))
        pulled[rows, :] = dot(coeff, items).astype(BF16)
        return total + jnp.sum(weight * losses)

    total = lax.fori_loop(0, queries.shape[0] // ROWS, softmax, jnp.zeros((), F32))

    def loss_send(stage, n, to):
        send(remote(loss_out.at[stage], loss_in.at[stage, n], lo_s.at[stage, n], lo_r.at[stage, n], to))

    def loss_sum(stage, count):
        value = loss_out[stage]
        for n in range(count):
            remote(
                loss_out.at[stage], loss_in.at[stage, n], lo_s.at[stage, n], lo_r.at[stage, n], sibling
            ).wait_recv()
            value = value + loss_in[stage, n]
        return value

    loss_out[0] = jnp.full((8, 128), total, F32)
    loss_send(0, 0, sibling)

    for copy in sent[:-1]:
        copy.wait_send()
    del sent[:-1]

    full = wall.shape[2]

    def unit(k, q):
        cols = pl.ds(pl.multiple_of(q * WIDE, WIDE), WIDE)
        upper = dot(hid_t[k], grad_q[:, cols])
        span = full - block_rows
        taken = pulled[:, pl.ds(pl.multiple_of(k * SIDE * span, SIDE * span), SIDE * span)]
        lower = dot(taken, queries[:, cols], (0, 0))
        return jnp.reshape(upper, (SIDE, block_rows, WIDE)), jnp.reshape(lower, (SIDE, span, WIDE))

    def sib_copy(p, k, c):
        four = pl.ds(k * SIDE, SIDE)
        return remote(
            wall.at[2 * c + p, four], sib_in.at[p, four], sib_s.at[p, k], sib_r.at[p, k], sibling
        )

    def fz_copy(o):
        four = pl.ds(((z + o) % SIDE) * SIDE, SIDE)
        return remote(wall.at[2 * core, four], first_z.at[o - 1], fz_s.at[o - 1], fz_r.at[o - 1], z_peer(o))

    def fy_copy(k, o):
        b = k * SIDE + (y + o) % SIDE
        n = o - 1
        return remote(wall.at[2 * core + 1, b], first_y.at[n, k], fy_s.at[n, k], fy_r.at[n, k], y_peer(o))

    def reduce_group(i, carry):
        k = (z + 1 + i) % SIDE
        four = pl.ds(k * SIDE, SIDE)
        for p in range(2):
            q = 2 * (1 - core) + p
            upper, lower = unit(k, q)
            wall[q, four, 0:block_rows, :] = upper.astype(BF16)
            wall[q, four, block_rows:full, :] = lower.astype(BF16)
            sib_copy(p, k, 1 - core).start()
        for p in range(2):
            q = 2 * core + p
            upper, lower = unit(k, q)
            sib_copy(p, k, 1 - core).wait_recv()
            wall[q, four, 0:block_rows, :] = (upper + sib_in[p, four, 0:block_rows, :].astype(F32)).astype(BF16)
            wall[q, four, block_rows:full, :] = (lower + sib_in[p, four, block_rows:full, :].astype(F32)).astype(BF16)
            if p == 0:
                @pl.when(i < SIDE - 1)
                def _():
                    b = pl.ds(k * SIDE, SIDE)
                    remote(
                        wall.at[2 * core, b], first_z.at[i], fz_s.at[i], fz_r.at[i],
                        device(k, y, high, core, low),
                    ).start()
            else:
                for o in (1, 2, 3):
                    fy_copy(k, o).start()
        return carry

    lax.fori_loop(0, SIDE, reduce_group, 0)

    loss_out[1] = loss_sum(0, 1)
    for o in (1, 2, 3):
        loss_send(1, o - 1, z_peer(o))

    def second_copy(p, o):
        if p == 0:
            b, to = z * SIDE + (y + o) % SIDE, y_peer(o)
        else:
            b, to = ((z + o) % SIDE) * SIDE + y, z_peer(o)
        return remote(
            wall.at[2 * core + p, b], second_in.at[p, o - 1], se_s.at[p, o - 1], se_r.at[p, o - 1], to
        )

    mine = [None, None]
    for o in (1, 2, 3):
        fz_copy(o).wait_recv()
    for o in (1, 2, 3, 0):
        yy = (y + o) % SIDE
        value = wall[2 * core, z * SIDE + yy].astype(F32)
        for n in range(3):
            value = value + first_z[n, yy].astype(F32)
        if o:
            wall[2 * core, z * SIDE + yy] = value.astype(BF16)
            second_copy(0, o).start()
        else:
            mine[0] = value
    for o in (1, 2, 3, 0):
        zz = (z + o) % SIDE
        b = zz * SIDE + y
        value = wall[2 * core + 1, b].astype(F32)
        for n in range(3):
            fy_copy(zz, n + 1).wait_recv()
            value = value + first_y[n, zz].astype(F32)
        if o:
            wall[2 * core + 1, b] = value.astype(BF16)
            second_copy(1, o).start()
        else:
            mine[1] = value

    loss_out[2] = loss_sum(1, 3)
    for o in (1, 2, 3):
        loss_send(2, o - 1, y_peer(o))

    tall = slot_out.shape[2]
    shape = (LINE * tall, full)
    row = lax.broadcasted_iota(jnp.int32, shape, 0)
    col = lax.broadcasted_iota(jnp.int32, shape, 1)
    owner = sum(jnp.where(row >= tall * s, 1, 0) for s in range(1, LINE))
    inner = row - tall * owner
    from_w = (inner < own_rows) & (col == own_rows * owner + inner)
    from_a = (inner >= 32) & (inner < 32 + adapter_rows) & (col == block_rows + adapter_rows * owner + inner - 32)
    spread = jnp.where(from_w | from_a, 1.0, 0.0).astype(BF16)
    for p in range(2):
        value = mine[p]
        for o in (1, 2, 3):
            second_copy(p, o).wait_recv()
            value = value + second_in[p, o - 1].astype(F32)
        slots = dot(spread, value.astype(BF16)).astype(BF16)
        slot_out[p] = jnp.reshape(slots, (LINE, tall, WIDE))

    def slot_copy(k):
        return remote(
            slot_out.at[:, line_slot(k)], slot_in.at[k], sl_s.at[k], sl_r.at[k], line_peer(k)
        )

    for k in (1, 4, 5, 3, 6, 7, 2):
        slot_copy(k).start()

    loss_out[3] = loss_sum(2, 3)
    for n, k in enumerate((1, 4, 5)):
        loss_send(3, n, line_peer(k))

    for k in range(1, LINE):
        slot_copy(k).wait_recv()
    for p in range(2):
        same = slot_out[p, slot].astype(F32)
        for k in (1, 4, 5):
            same = same + slot_in[k, p].astype(F32)
        other = slot_in[2, p].astype(F32)
        for k in (3, 6, 7):
            other = other + slot_in[k, p].astype(F32)
        for value, c in ((same, core), (other, 1 - core)):
            cols = pl.ds(pl.multiple_of((2 * c + p) * WIDE, WIDE), WIDE)
            gw_ref[:, cols] = value[0:own_rows]
            ga_ref[:, cols] = scale * value[32:32 + adapter_rows]

    loss_ref[...] = loss_sum(3, 3)

    for copy in sent:
        copy.wait_send()
    for p in range(2):
        for k in range(SIDE):
            sib_copy(p, k, 1 - core).wait_send()
    for o in (1, 2, 3):
        fz_copy(o).wait_send()
        for k in range(SIDE):
            fy_copy(k, o).wait_send()
        for p in range(2):
            second_copy(p, o).wait_send()
    for k in range(1, LINE):
        slot_copy(k).wait_send()


def on_device(hidden, w_query, adapter, item_emb, counts, positive, loss_weight):
    scale = 2.0 / math.sqrt(adapter.shape[0])
    devices = lax.axis_size(AXES)
    queries, deep = hidden.shape
    wide = adapter.shape[0]
    items = counts.shape[0]
    block = LINE * w_query.shape[0]
    full = block + LINE * (wide // devices)
    sem = pltpu.SemaphoreType.DMA
    vmem = pl.BlockSpec(memory_space=pltpu.VMEM)
    anywhere = pl.BlockSpec(memory_space=pl.ANY)
    gw, ga, loss = pl.pallas_call(
        functools.partial(step_kernel, scale),
        out_shape=(
            jax.ShapeDtypeStruct((w_query.shape[0], wide), F32),
            jax.ShapeDtypeStruct((wide // devices, wide), F32),
            jax.ShapeDtypeStruct((8, 128), F32),
        ),
        in_specs=[anywhere, vmem, anywhere, vmem, vmem, vmem, vmem],
        out_specs=(vmem, vmem, vmem),
        scratch_shapes=[
            pltpu.VMEM((SIDE, queries, deep // SIDE), BF16),
            pltpu.VMEM((SIDE, deep // SIDE, queries), BF16),
            pltpu.VMEM((wide, wide), BF16),
            pltpu.VMEM((QUARTERS, 16, full, WIDE), BF16),
            pltpu.VMEM((LINE, QUARTERS, 32, WIDE), BF16),
            pltpu.VMEM((SIDE, SIDE, LINE, items // devices, wide), BF16),
            pltpu.VMEM((items, wide), BF16),
            pltpu.VMEM((queries, wide), BF16),
            pltpu.VMEM((queries, wide), BF16),
            pltpu.VMEM((queries, wide), BF16),
            pltpu.VMEM((queries, 128), F32),
            pltpu.VMEM((queries, 128), F32),
            pltpu.VMEM((1, items), F32),
            pltpu.VMEM((2, 16, full, WIDE), BF16),
            pltpu.VMEM((3, SIDE, full, WIDE), BF16),
            pltpu.VMEM((3, SIDE, full, WIDE), BF16),
            pltpu.VMEM((2, 3, full, WIDE), BF16),
            pltpu.VMEM((2, LINE, 48, WIDE), BF16),
            pltpu.VMEM((LINE, 2, 48, WIDE), BF16),
            pltpu.VMEM((4, 8, 128), F32),
            pltpu.VMEM((4, 3, 8, 128), F32),
            sem((SIDE + 1,)),
            sem((LINE,)), sem((LINE,)),
            sem((2, 16)), sem((2, 16)),
            sem((2, 16)), sem((2, 16)),
            sem((13,)), sem((13,)),
            sem((2, SIDE)), sem((2, SIDE)),
            sem((3,)), sem((3,)),
            sem((3, SIDE)), sem((3, SIDE)),
            sem((2, 3)), sem((2, 3)),
            sem((LINE,)), sem((LINE,)),
            sem((4, 3)), sem((4, 3)),
        ],
        compiler_params=pltpu.CompilerParams(
            collective_id=0, has_side_effects=True, vmem_limit_bytes=64 * 1024 * 1024 - 65536
        ),
        name="sampled_softmax_step",
    )(
        hidden, w_query, adapter, item_emb, counts.reshape(1, items),
        positive.reshape(queries // 128, 128), loss_weight.reshape(queries // 128, 128),
    )
    return gw, ga, loss[0, 0] / (queries * devices)


def solution(mesh):
    placed = (P(AXES, None), P(AXES, None), P(), P(AXES, None), P(), P(AXES), P(AXES))
    return jax.shard_map(
        on_device,
        mesh=mesh,
        in_specs=placed,
        out_specs=(P(AXES, None), P(AXES, None), P()),
        check_vma=False,
    )
```

time: 2130 us -> 142 us (0.07)
  waiting for transfers between devices: 1960 us -> 0 us
  Pallas kernels: 0 us -> 135 us
  blocking collectives: 67.4 us -> 0 us
  matrix products: 62.2 us -> 0 us
    unnamed x7 -> x0, waiting for transfers between devices: 737 us -> none
    reduce_scatter x1 -> x0, waiting for transfers between devices: 621 us -> none  [on_device(): lax.psum_scatter(scale * jnp.einsum('qn,qe->ne', coeff, queries, preferre...]
    all_gather x2 -> x0, waiting for transfers between devices: 599 us -> none  [the longest x1 314 us: on_device(): whole_weight = lax.all_gather(w_query, ('item', 'qgrp'), axis=0, tiled=True)]
    pallas_call x0 -> x1, Pallas kernels: none -> 135 us  [on_device(): pl.pallas_call(functools.partial(step_kernel, scale), out_shape=(jax.Shap...]
    psum x1 -> x0, blocking collectives: 67.4 us -> none  [on_device(): total = lax.psum(jnp.sum(loss_weight * losses), ('item', 'qgrp'))]
    dot_general x6 -> x0, matrix products: 62.2 us -> none  [the longest x1 25.2 us: on_device(): jnp.einsum('qh,qe->he', hidden, grad_q, preferred_element_type=jnp.float32)]
  transfers between devices with their start and end apart: 5 -> 0, of which waited for: 5 -> 0; matrix products, arithmetic and copies ran while one was open for 3% -> 0% of each run, Pallas kernels for 0% -> 0%
where the time goes in v1:
time: 142 us; the launch traced here: 141 us
  Pallas kernels  135 us (95%)
  local copies, waits for them, and re-layouts  4.13 us (3%)
  between operations  2.42 us (2%)
    pallas_call x1, Pallas kernels, on_device(): pl.pallas_call(functools.partial(step_kernel, scale), out_shape=(jax.Shap...  135 us
    unnamed x2, local copies, waits for them, and re-layouts  2.94 us

profile of v1, /device:TPU:1, one launch (start us, length us, event | category | flops | bytes accessed | tf_op | source)
XLA Modules:
  0.0 141.3 jit_solution(978743224981725841)
XLA Ops:
  0.6 134.7 %sampled_softmax_step.1 = (f32[28,1024]{1,0:T(8,128)}, f32[8,1024]{1,0:T(8,128)}, f32[8,128]{1,0:T(8,128)}) custom-call(bf16[1024,3584]{1,0:T(8,128)(2,1)} %hidden_ref.1, bf16[28,1024]{1,0:T(8,128)(2,1)} %w_ref.1, bf16[1024,1024]{1,0:T(8,128)(2,1)} %adapter_ref.1, bf16[16,1024]{1,0:T(8,128)(2,1)} %item_ref.1, s32[1,2048]{1,0:T(1,128)} %bitcast.4, ...), custom_call_target="tpu_custom_call" | custom-call | tf_op jit(solution)/shard_map/sampled_softmax_step/pallas_call | solution.py:455
  135.3 1.2 slice.3
  137.2 1.6 %copy.12 = f32[28,1024]{1,0:T(8,128)} copy(f32[28,1024]{1,0:T(8,128)} %get-tuple-element.12) | data formatting | bytes 229376
  138.8 1.4 copy.13

commit v2 on v1

--- a/solution.py
+++ b/solution.py
@@ -40,9 +40,9 @@
 def step_kernel(
     scale, hidden_ref, w_ref, adapter_ref, item_ref, counts_ref, positive_ref, weight_ref,
     gw_ref, ga_ref, loss_ref,
-    hid, hid_t, ada, wall, xs, pool, adapted, queries, grad_q, pulled, pos_col, weight_col, log_count,
+    hid, hid_t, ada, wall, xs, pool, adapted, partial, queries, coeff, grad_q, pulled, pos_col, weight_col, log_count,
     sib_in, first_z, first_y, second_in, slot_out, slot_in, loss_out, loss_in,
-    load_sem, xs_s, xs_r, w_s, w_r, ws_s, ws_r, e_s, e_r, sib_s, sib_r, fz_s, fz_r, fy_s, fy_r, se_s, se_r,
+    load_sem, xs_s, xs_r, w_s, w_r, ws_s, ws_r, ez_s, ez_r, ey_s, ey_r, ex_s, ex_r, es_s, es_r, sib_s, sib_r, fz_s, fz_r, fy_s, fy_r, se_s, se_r,
     sl_s, sl_r, lo_s, lo_r,
 ):
     z, y, high, core, low = place()
@@ -56,6 +56,10 @@
     def z_peer(o):
         return device((z + o) % SIDE, y, high, core, low)
 
+    def x_peer(o):
+        xx = (2 * high + low + o) % SIDE
+        return device(z, y, xx // 2, core, xx % 2)
+
     def y_peer(o):
         return device(z, (y + o) % SIDE, high, core, low)
 
@@ -106,7 +110,7 @@
         send(remote(xs.at[slot, pair], xs.at[slot, pair], xs_s.at[k], xs_r.at[k], line_peer(k)))
     own_e = pool.at[z, y, slot]
     for o in (1, 2, 3):
-        send(remote(own_e, own_e, e_s.at[o - 1], e_r.at[o - 1], z_peer(o)))
+        send(remote(own_e, own_e, ez_s.at[o - 1], ez_r.at[o - 1], z_peer(o)))
 
     log_count[...] = jnp.log(counts_ref[...].astype(F32))
     for r in range(positive_ref.shape[0]):
@@ -115,12 +119,30 @@
         pos_col[rows, :] = jnp.broadcast_to(line, (128, 128)).T
         weight_col[rows, :] = jnp.broadcast_to(weight_ref[r:r + 1, :], (128, 128)).T
 
+    def e_column(o, ox, c):
+        xx = (2 * high + low - ox + SIDE) % SIDE
+        return pool.at[:, (y - o + SIDE) % SIDE, (xx // 2) * 4 + c * 2 + xx % 2]
+
+    def e_along(o, ox, new_ox, to):
+        at = e_column(o, ox, core)
+        send(remote(at, at, ex_s.at[new_ox - 1, o], ex_r.at[new_ox - 1, o], x_peer(to)))
+
+    def e_share(o, ox):
+        at = e_column(o, ox, core)
+        send(remote(at, at, es_s.at[ox, o], es_r.at[ox, o], sibling))
+
+    def e_wait_x(o, ox):
+        at = e_column(o, ox, core)
+        remote(at, at, ex_s.at[ox - 1, o], ex_r.at[ox - 1, o], sibling).wait_recv()
+
     for o in (1, 2, 3):
         got = pool.at[(z - o + SIDE) % SIDE, y, slot]
-        remote(got, got, e_s.at[o - 1], e_r.at[o - 1], z_peer(o)).wait_recv()
-    column_e = pool.at[:, y, slot]
-    for o in (1, 2, 3):
-        send(remote(column_e, column_e, e_s.at[2 + o], e_r.at[2 + o], y_peer(o)))
+        remote(got, got, ez_s.at[o - 1], ez_r.at[o - 1], z_peer(o)).wait_recv()
+    own_column = e_column(0, 0, core)
+    for o in (1, 3, 2):
+        send(remote(own_column, own_column, ey_s.at[o - 1], ey_r.at[o - 1], y_peer(o)))
+    for o in (1, 3):
+        e_along(0, 0, o, o)
 
     for k in range(1, LINE):
         got = xs.at[line_slot(k), pl.ds(2 * core, 2)]
@@ -169,48 +191,75 @@
     for o in (1, 3, 2):
         for p in range(2):
             w_send(p, 0, 0, o, 0, near[p][0](o))
-    for o in (1, 3, 2):
+    for o in (1, 3):
         for p in range(2):
             w_send(p, 0, 0, 0, o, near[p][1](o))
     for p in range(2):
         w_share(p, 0, 0)
-
-    for o in (1, 2, 3):
-        got = pool.at[:, (y - o + SIDE) % SIDE, slot]
-        remote(got, got, e_s.at[2 + o], e_r.at[2 + o], y_peer(o)).wait_recv()
-    slab = pool.at[:, :, slot]
-    for n, k in enumerate((1, 4, 5)):
-        send(remote(slab, slab, e_s.at[6 + n], e_r.at[6 + n], line_peer(k)))
-    send(remote(slab, slab, e_s.at[9], e_r.at[9], sibling))
-
-    for of in (1, 3, 2):
-        for p in range(2):
-            w_wait(p, of, 0)
-            for og in (1, 3, 2):
-                w_send(p, of, 0, of, og, near[p][1](og))
-            w_share(p, of, 0)
-
-    for k in range(SIDE):
+    e_share(0, 0)
+
+    def transpose(k):
         loads[k].wait()
         for s in range(group // 128):
             hid_t[k, 128 * s:128 * (s + 1), :] = hid[k, :, 128 * s:128 * (s + 1)].T
-        if k == 1:
-            for p in range(2):
-                for og in (1, 3, 2):
-                    w_wait(p, 0, og)
-                    w_share(p, 0, og)
-    for n, k in enumerate((1, 4, 5)):
-        got = pool.at[:, :, line_slot(k)]
-        remote(got, got, e_s.at[6 + n], e_r.at[6 + n], line_peer(k)).wait_recv()
-        send(remote(got, got, e_s.at[10 + n], e_r.at[10 + n], sibling))
-    for p in range(2):
-        for of in (1, 3, 2):
-            for og in (1, 3, 2):
-                w_wait(p, of, og)
-                w_share(p, of, og)
-    for n, k in enumerate((2, 3, 6, 7)):
-        got = pool.at[:, :, line_slot(k)]
-        remote(got, got, e_s.at[9 + n], e_r.at[9 + n], sibling).wait_recv()
+
+    transpose(0)
+    for o in (1, 3, 2):
+        got = e_column(o, 0, core)
+        remote(got, got, ey_s.at[o - 1], ey_r.at[o - 1], y_peer(o)).wait_recv()
+        for ox in (1, 3):
+            e_along(o, 0, ox, ox)
+        e_share(o, 0)
+    for of in (1, 3, 2):
+        for p in range(2):
+            w_wait(p, of, 0)
+            for og in (1, 3):
+                w_send(p, of, 0, of, og, near[p][1](og))
+            w_share(p, of, 0)
+    transpose(1)
+
+    for n, o in enumerate((0, 1, 3, 2)):
+        for ox in (1, 3):
+            e_wait_x(o, ox)
+            if ox == (1 if n < 2 else 3):
+                e_along(o, ox, 2, 1 if ox == 1 else 3)
+            e_share(o, ox)
+        for p in range(2):
+            for og in (1, 3):
+                w_wait(p, o, og)
+                if og == (1 if n < 2 else 3):
+                    w_send(p, o, og, o, 2, near[p][1](og))
+                w_share(p, o, og)
+        if n < 2:
+            transpose(2 + n)
+
+    def w_got(p, of, og):
+        at = w_at(p, of, og, 1 - core)
+        n = of * SIDE + og
+        remote(at, at, ws_s.at[p, n], ws_r.at[p, n], sibling).wait_recv()
+
+    def project(q, offset):
+        k = (z - offset + SIDE) % SIDE
+        part = jnp.reshape(wall[q, pl.ds(SIDE * k, SIDE), 0:block_rows, :], (group, WIDE))
+        return dot(hid[k], part)
+
+    own_first, sib_first = 2 * core, 2 * (1 - core)
+    partial[0] = project(own_first, 0) + project(own_first, 1) + project(own_first, 3)
+    for of in (0, 1, 3, 2):
+        for og in (0, 1, 3):
+            w_got(0, of, og)
+    partial[1] = project(sib_first, 0) + project(sib_first, 1) + project(sib_first, 3)
+
+    for o in (0, 1, 3, 2):
+        e_wait_x(o, 2)
+        e_share(o, 2)
+        for p in range(2):
+            w_wait(p, o, 2)
+            w_share(p, o, 2)
+    for ox in range(SIDE):
+        for o in range(SIDE):
+            got = e_column(o, ox, 1 - core)
+            remote(got, got, es_s.at[ox, o], es_r.at[ox, o], sibling).wait_recv()
 
     loads[SIDE].wait()
     chunk = pool.shape[2] * pool.shape[3] * 2
@@ -223,24 +272,20 @@
 
     lax.fori_loop(0, adapted.shape[0] // chunk, adapt, 0)
 
-    for p in range(2):
-        for of in range(SIDE):
-            for og in range(SIDE):
-                at = w_at(p, of, og, 1 - core)
-                n = of * SIDE + og
-                remote(at, at, ws_s.at[p, n], ws_r.at[p, n], sibling).wait_recv()
-
-    def project(i, carry):
-        cols = pl.ds(pl.multiple_of(i * WIDE, WIDE), WIDE)
-        total = None
-        for k in range(SIDE):
-            part = jnp.reshape(wall[i, SIDE * k:SIDE * (k + 1), 0:block_rows, :], (group, WIDE))
-            term = dot(hid[k], part)
-            total = term if total is None else total + term
-        queries[:, cols] = total.astype(BF16)
-        return carry
-
-    lax.fori_loop(0, QUARTERS, project, 0)
+    def columns(q):
+        return pl.ds(pl.multiple_of(q * WIDE, WIDE), WIDE)
+
+    queries[:, columns(own_first)] = (partial[0] + project(own_first, 2)).astype(BF16)
+    own_next = sum(project(own_first + 1, o) for o in range(SIDE))
+    queries[:, columns(own_first + 1)] = own_next.astype(BF16)
+    for of in range(SIDE):
+        w_got(0, of, 2)
+    queries[:, columns(sib_first)] = (partial[1] + project(sib_first, 2)).astype(BF16)
+    for of in range(SIDE):
+        for og in range(SIDE):
+            w_got(1, of, og)
+    sib_next = sum(project(sib_first + 1, o) for o in range(SIDE))
+    queries[:, columns(sib_first + 1)] = sib_next.astype(BF16)
 
     items_all = adapted.shape[0]
 
@@ -256,10 +301,9 @@
         weight = weight_col[rows, 0:1]
         losses = jnp.log(denom) + top - picked
         plain = shifted * (weight / denom)
-        coeff = jnp.where(hit, plain - weight, plain).astype(BF16)
-        grad_q[rows, :] = (scale * dot(coeff, adapted[...])).astype(BF16)
-        items = jnp.reshape(pool[...], (items_all, pool.shape[4]))
-        pulled[rows, :] = dot(coeff, items).astype(BF16)
+        part = jnp.where(hit, plain - weight, plain).astype(BF16)
+        coeff[rows, :] = part
+        grad_q[rows, :] = (scale * dot(part, adapted[...])).astype(BF16)
         return total + jnp.sum(weight * losses)
 
     total = lax.fori_loop(0, queries.shape[0] // ROWS, softmax, jnp.zeros((), F32))
@@ -284,13 +328,12 @@
     del sent[:-1]
 
     full = wall.shape[2]
+    span = full - block_rows
 
     def unit(k, q):
-        cols = pl.ds(pl.multiple_of(q * WIDE, WIDE), WIDE)
+        cols = columns(q)
         upper = dot(hid_t[k], grad_q[:, cols])
-        span = full - block_rows
-        taken = pulled[:, pl.ds(pl.multiple_of(k * SIDE * span, SIDE * span), SIDE * span)]
-        lower = dot(taken, queries[:, cols], (0, 0))
+        lower = dot(pulled[...], queries[:, cols])
         return jnp.reshape(upper, (SIDE, block_rows, WIDE)), jnp.reshape(lower, (SIDE, span, WIDE))
 
     def sib_copy(p, k, c):
@@ -311,6 +354,8 @@
     def reduce_group(i, carry):
         k = (z + 1 + i) % SIDE
         four = pl.ds(k * SIDE, SIDE)
+        some = pool[:, :, :, :, pl.ds(pl.multiple_of(k * SIDE * span, SIDE * span), SIDE * span)]
+        pulled[...] = dot(coeff[...], jnp.reshape(some, (items_all, SIDE * span))).T.astype(BF16)
         for p in range(2):
             q = 2 * (1 - core) + p
             upper, lower = unit(k, q)
@@ -439,6 +484,12 @@
             second_copy(p, o).wait_send()
     for k in range(1, LINE):
         slot_copy(k).wait_send()
+
+
+def finish_kernel(share, gw_in, ga_in, loss_in, gw_ref, ga_ref, loss_ref):
+    gw_ref[...] = gw_in[...]
+    ga_ref[...] = ga_in[...]
+    loss_ref[...] = loss_in[0:1, 0:1] * share
 
 
 def on_device(hidden, w_query, adapter, item_emb, counts, positive, loss_weight):
@@ -469,9 +520,11 @@
             pltpu.VMEM((LINE, QUARTERS, 32, WIDE), BF16),
             pltpu.VMEM((SIDE, SIDE, LINE, items // devices, wide), BF16),
             pltpu.VMEM((items, wide), BF16),
+            pltpu.VMEM((2, queries, WIDE), F32),
             pltpu.VMEM((queries, wide), BF16),
+            pltpu.VMEM((queries, items), BF16),
             pltpu.VMEM((queries, wide), BF16),
-            pltpu.VMEM((queries, wide), BF16),
+            pltpu.VMEM((wide // SIDE, queries), BF16),
             pltpu.VMEM((queries, 128), F32),
             pltpu.VMEM((queries, 128), F32),
             pltpu.VMEM((1, items), F32),
@@ -487,7 +540,10 @@
             sem((LINE,)), sem((LINE,)),
             sem((2, 16)), sem((2, 16)),
             sem((2, 16)), sem((2, 16)),
-            sem((13,)), sem((13,)),
+            sem((3,)), sem((3,)),
+            sem((3,)), sem((3,)),
+            sem((3, SIDE)), sem((3, SIDE)),
+            sem((SIDE, SIDE)), sem((SIDE, SIDE)),
             sem((2, SIDE)), sem((2, SIDE)),
             sem((3,)), sem((3,)),
             sem((3, SIDE)), sem((3, SIDE)),
@@ -503,7 +559,18 @@
         hidden, w_query, adapter, item_emb, counts.reshape(1, items),
         positive.reshape(queries // 128, 128), loss_weight.reshape(queries // 128, 128),
     )
-    return gw, ga, loss[0, 0] / (queries * devices)
+    gw, ga, loss = pl.pallas_call(
+        functools.partial(finish_kernel, 1.0 / (queries * devices)),
+        out_shape=(
+            jax.ShapeDtypeStruct(gw.shape, F32),
+            jax.ShapeDtypeStruct(ga.shape, F32),
+            jax.ShapeDtypeStruct((1, 1), F32),
+        ),
+        in_specs=[vmem, vmem, vmem],
+        out_specs=(vmem, vmem, vmem),
+        name="finish",
+    )(gw, ga, loss)
+    return gw, ga, loss.reshape(())
 
 
 def solution(mesh):

time: 142 us -> 135 us (0.951)
  local copies, waits for them, and re-layouts: 4.13 us -> 0 us
  between operations: 2.42 us -> 0.64 us
    unnamed x2 -> x0, local copies, waits for them, and re-layouts: 2.94 us -> none
    pallas_call x1, Pallas kernels: 135 us -> 133 us  [on_device(): pl.pallas_call(functools.partial(step_kernel, scale), out_shape=(jax.Shap...]
    pallas_call x0 -> x1, Pallas kernels: none -> 1.6 us  [on_device(): pl.pallas_call(functools.partial(finish_kernel, 1.0 / (queries * devices)...]
where the time goes in v2:
time: 135 us
  Pallas kernels  134 us (99%)
    pallas_call x1, Pallas kernels, on_device(): pl.pallas_call(functools.partial(step_kernel, scale), out_shape=(jax.Shap...  133 us

profile of v2, /device:TPU:1, one launch (start us, length us, event | category | flops | bytes accessed | tf_op | source)
XLA Modules:
  0.0 135.1 jit_solution(10534635753087089066)
XLA Ops:
  0.6 132.8 %sampled_softmax_step.1 = (f32[28,1024]{1,0:T(8,128)}, f32[8,1024]{1,0:T(8,128)}, f32[8,128]{1,0:T(8,128)}) custom-call(bf16[1024,3584]{1,0:T(8,128)(2,1)} %hidden_ref.1, bf16[28,1024]{1,0:T(8,128)(2,1)} %w_ref.1, bf16[1024,1024]{1,0:T(8,128)(2,1)} %adapter_ref.1, bf16[16,1024]{1,0:T(8,128)(2,1)} %item_ref.1, s32[1,2048]{1,0:T(1,128)} %bitcast.4, ...), custom_call_target="tpu_custom_call" | custom-call | tf_op jit(solution)/shard_map/sampled_softmax_step/pallas_call | solution.py:506
  133.5 1.6 %finish.1 = (f32[28,1024]{1,0:T(8,128)}, f32[8,1024]{1,0:T(8,128)}, f32[1,1]{1,0:T(1,128)}) custom-call(f32[28,1024]{1,0:T(8,128)} %get-tuple-element.9.gw_in, f32[8,1024]{1,0:T(8,128)} %get-tuple-element.10.ga_in, f32[8,128]{1,0:T(8,128)} %get-tuple-element.11.loss_in), custom_call_target="tpu_custom_call" | custom-call | tf_op jit(solution)/shard_map/finish/pallas_call | solution.py:562

commit v3 on v2

--- a/solution.py
+++ b/solution.py
@@ -40,7 +40,7 @@
 def step_kernel(
     scale, hidden_ref, w_ref, adapter_ref, item_ref, counts_ref, positive_ref, weight_ref,
     gw_ref, ga_ref, loss_ref,
-    hid, hid_t, ada, wall, xs, pool, adapted, partial, queries, coeff, grad_q, pulled, pos_col, weight_col, log_count,
+    hid, hid_t, wall, xs, pool, adapted, partial, queries, coeff, grad_q, pulled, pos_col, weight_col, log_count,
     sib_in, first_z, first_y, second_in, slot_out, slot_in, loss_out, loss_in,
     load_sem, xs_s, xs_r, w_s, w_r, ws_s, ws_r, ez_s, ez_r, ey_s, ey_r, ex_s, ex_r, es_s, es_r, sib_s, sib_r, fz_s, fz_r, fy_s, fy_r, se_s, se_r,
     sl_s, sl_r, lo_s, lo_r,
@@ -80,12 +80,14 @@
         )
 
     loads = [
-        pltpu.make_async_copy(hidden_ref.at[:, pl.ds(group * k, group)], hid.at[k], load_sem.at[k])
+        pltpu.make_async_copy(
+            hidden_ref.at[:, pl.ds(group * k, group)], coeff.at[:, pl.ds(group * (k % 2), group)], load_sem.at[k]
+        )
         for k in range(SIDE)
     ]
-    loads.append(pltpu.make_async_copy(adapter_ref, ada, load_sem.at[SIDE]))
-    for load in loads:
-        load.start()
+    loads.append(pltpu.make_async_copy(adapter_ref, grad_q, load_sem.at[SIDE]))
+    for k in (0, 1, SIDE):
+        loads[k].start()
 
     barrier = pltpu.get_barrier_semaphore()
     peers = [line_peer(k) for k in range(1, LINE)]
@@ -97,6 +99,7 @@
     for q in range(QUARTERS):
         xs[slot, q, 0:own_rows, :] = w_ref[:, q * WIDE:(q + 1) * WIDE]
     pool[z, y, slot] = item_ref[...]
+    padding = WIDE - block_rows
     pl.semaphore_wait(barrier, len(peers))
 
     sent = []
@@ -144,6 +147,23 @@
     for o in (1, 3):
         e_along(0, 0, o, o)
 
+    def split(k):
+        loads[k].wait()
+        for n in range(SIDE):
+            first = group * (k % 2) + block_rows * n
+            hid[SIDE * k + n, :, 0:block_rows] = coeff[:, first:first + block_rows]
+            hid[SIDE * k + n, :, block_rows:] = jnp.zeros((coeff.shape[0], padding), BF16)
+        if k + 2 < SIDE:
+            loads[k + 2].start()
+        for n in range(SIDE):
+            top = block_rows * n
+            hid_t[k, top:top + 128, :] = hid[SIDE * k + n, :, 0:128].T
+            hid_t[k, top + 128:top + block_rows, :] = hid[SIDE * k + n, :, 128:256].T[0:block_rows - 128]
+
+    split(0)
+    for q in range(QUARTERS):
+        wall[q, :, block_rows:WIDE, :] = jnp.zeros((wall.shape[1], padding, WIDE), BF16)
+
     for k in range(1, LINE):
         got = xs.at[line_slot(k), pl.ds(2 * core, 2)]
         remote(got, got, xs_s.at[k], xs_r.at[k], line_peer(k)).wait_recv()
@@ -198,12 +218,7 @@
         w_share(p, 0, 0)
     e_share(0, 0)
 
-    def transpose(k):
-        loads[k].wait()
-        for s in range(group // 128):
-            hid_t[k, 128 * s:128 * (s + 1), :] = hid[k, :, 128 * s:128 * (s + 1)].T
-
-    transpose(0)
+    split(1)
     for o in (1, 3, 2):
         got = e_column(o, 0, core)
         remote(got, got, ey_s.at[o - 1], ey_r.at[o - 1], y_peer(o)).wait_recv()
@@ -216,82 +231,116 @@
             for og in (1, 3):
                 w_send(p, of, 0, of, og, near[p][1](og))
             w_share(p, of, 0)
-    transpose(1)
-
-    for n, o in enumerate((0, 1, 3, 2)):
+    split(2)
+    split(3)
+
+    def w_got(p, of, og):
+        at = w_at(p, of, og, 1 - core)
+        n = of * SIDE + og
+        remote(at, at, ws_s.at[p, n], ws_r.at[p, n], sibling).wait_recv()
+
+    half_rows = hid.shape[1] // 2
+
+    def project(p, c, og):
+        q = 2 * c + p
+        blocks = [w_block(p, of, og) for of in range(SIDE)]
+
+        def rows_of(i, carry):
+            rows = pl.ds(pl.multiple_of(i * half_rows, half_rows), half_rows)
+            left = jnp.concatenate([hid[b, rows, :] for b in blocks], axis=1)
+            right = jnp.concatenate([wall[q, b, 0:WIDE, :] for b in blocks], axis=0)
+            value = dot(left, right)
+            if og == 0:
+                partial[q, rows, :] = value
+            elif og == 2:
+                queries[rows, columns(q)] = (partial[q, rows, :] + value).astype(BF16)
+            else:
+                partial[q, rows, :] += value
+            return carry
+
+        lax.fori_loop(0, 2, rows_of, 0)
+
+    def columns(q):
+        return pl.ds(pl.multiple_of(q * WIDE, WIDE), WIDE)
+
+    def adapt(o):
+        yy = (y - o + SIDE) % SIDE
+        items = jnp.reshape(pool[:, yy], (SIDE * LINE * item_ref.shape[0], queries.shape[1]))
+        value = (items.astype(F32) + dot(items, grad_q[...])).astype(BF16)
+        adapted[:, yy] = jnp.reshape(value, (SIDE, LINE * item_ref.shape[0], queries.shape[1]))
+
+    def finish_items(o):
+        e_wait_x(o, 2)
+        e_share(o, 2)
+        for ox in range(SIDE):
+            got = e_column(o, ox, 1 - core)
+            remote(got, got, es_s.at[ox, o], es_r.at[ox, o], sibling).wait_recv()
+        adapt(o)
+
+    loads[SIDE].wait()
+    order = (0, 1, 3, 2)
+    for n, o in enumerate(order):
+        for p in range(2):
+            for og in (1, 3):
+                w_wait(p, o, og)
+                if og == (1 if n < 2 else 3):
+                    w_send(p, o, og, o, 2, near[p][1](og))
+                w_share(p, o, og)
         for ox in (1, 3):
             e_wait_x(o, ox)
             if ox == (1 if n < 2 else 3):
                 e_along(o, ox, 2, 1 if ox == 1 else 3)
             e_share(o, ox)
-        for p in range(2):
-            for og in (1, 3):
-                w_wait(p, o, og)
-                if og == (1 if n < 2 else 3):
-                    w_send(p, o, og, o, 2, near[p][1](og))
-                w_share(p, o, og)
-        if n < 2:
-            transpose(2 + n)
-
-    def w_got(p, of, og):
-        at = w_at(p, of, og, 1 - core)
-        n = of * SIDE + og
-        remote(at, at, ws_s.at[p, n], ws_r.at[p, n], sibling).wait_recv()
-
-    def project(q, offset):
-        k = (z - offset + SIDE) % SIDE
-        part = jnp.reshape(wall[q, pl.ds(SIDE * k, SIDE), 0:block_rows, :], (group, WIDE))
-        return dot(hid[k], part)
-
-    own_first, sib_first = 2 * core, 2 * (1 - core)
-    partial[0] = project(own_first, 0) + project(own_first, 1) + project(own_first, 3)
-    for of in (0, 1, 3, 2):
-        for og in (0, 1, 3):
-            w_got(0, of, og)
-    partial[1] = project(sib_first, 0) + project(sib_first, 1) + project(sib_first, 3)
-
-    for o in (0, 1, 3, 2):
-        e_wait_x(o, 2)
-        e_share(o, 2)
+        if n == 0:
+            for p in range(2):
+                project(p, core, 0)
+        if n == 1:
+            for p in range(2):
+                for of in range(SIDE):
+                    w_got(p, of, 0)
+                project(p, 1 - core, 0)
+        if n >= 2:
+            finish_items(order[n - 2])
+
+    def last(o):
         for p in range(2):
             w_wait(p, o, 2)
             w_share(p, o, 2)
-    for ox in range(SIDE):
-        for o in range(SIDE):
-            got = e_column(o, ox, 1 - core)
-            remote(got, got, es_s.at[ox, o], es_r.at[ox, o], sibling).wait_recv()
-
-    loads[SIDE].wait()
-    chunk = pool.shape[2] * pool.shape[3] * 2
-
-    def adapt(i, carry):
-        rows = pl.ds(pl.multiple_of(i * chunk, chunk), chunk)
-        items = jnp.reshape(pool[i // 2, pl.ds((i % 2) * 2, 2)], (chunk, pool.shape[4]))
-        adapted[rows, :] = (items.astype(F32) + dot(items, ada[...])).astype(BF16)
-        return carry
-
-    lax.fori_loop(0, adapted.shape[0] // chunk, adapt, 0)
-
-    def columns(q):
-        return pl.ds(pl.multiple_of(q * WIDE, WIDE), WIDE)
-
-    queries[:, columns(own_first)] = (partial[0] + project(own_first, 2)).astype(BF16)
-    own_next = sum(project(own_first + 1, o) for o in range(SIDE))
-    queries[:, columns(own_first + 1)] = own_next.astype(BF16)
-    for of in range(SIDE):
-        w_got(0, of, 2)
-    queries[:, columns(sib_first)] = (partial[1] + project(sib_first, 2)).astype(BF16)
-    for of in range(SIDE):
-        for og in range(SIDE):
-            w_got(1, of, og)
-    sib_next = sum(project(sib_first + 1, o) for o in range(SIDE))
-    queries[:, columns(sib_first + 1)] = sib_next.astype(BF16)
-
-    items_all = adapted.shape[0]
+
+    for p in range(2):
+        project(p, core, 1)
+    last(0)
+    for p in range(2):
+        project(p, core, 3)
+    last(1)
+    finish_items(3)
+    last(3)
+    for p in range(2):
+        for of in range(SIDE):
+            w_got(p, of, 1)
+        project(p, 1 - core, 1)
+    last(2)
+    for p in range(2):
+        for of in range(SIDE):
+            w_got(p, of, 3)
+        project(p, 1 - core, 3)
+    finish_items(2)
+
+    for p in range(2):
+        project(p, core, 2)
+    for p in range(2):
+        for of in range(SIDE):
+            w_got(p, of, 2)
+        project(p, 1 - core, 2)
+
+    items_all = log_count.shape[1]
+
+    def all_adapted():
+        return jnp.reshape(adapted[...], (items_all, queries.shape[1]))
 
     def softmax(i, total):
         rows = pl.ds(pl.multiple_of(i * ROWS, ROWS), ROWS)
-        logits = scale * dot(queries[rows, :], adapted[...], (1, 1)) - log_count[...]
+        logits = scale * dot(queries[rows, :], all_adapted(), (1, 1)) - log_count[...]
         top = jnp.max(logits, axis=1, keepdims=True)
         shifted = jnp.exp(logits - top)
         denom = jnp.sum(shifted, axis=1, keepdims=True)
@@ -303,7 +352,7 @@
         plain = shifted * (weight / denom)
         part = jnp.where(hit, plain - weight, plain).astype(BF16)
         coeff[rows, :] = part
-        grad_q[rows, :] = (scale * dot(part, adapted[...])).astype(BF16)
+        grad_q[rows, :] = (scale * dot(part, all_adapted())).astype(BF16)
         return total + jnp.sum(weight * losses)
 
     total = lax.fori_loop(0, queries.shape[0] // ROWS, softmax, jnp.zeros((), F32))
@@ -513,14 +562,13 @@
         in_specs=[anywhere, vmem, anywhere, vmem, vmem, vmem, vmem],
         out_specs=(vmem, vmem, vmem),
         scratch_shapes=[
-            pltpu.VMEM((SIDE, queries, deep // SIDE), BF16),
+            pltpu.VMEM((16, queries, WIDE), BF16),
             pltpu.VMEM((SIDE, deep // SIDE, queries), BF16),
-            pltpu.VMEM((wide, wide), BF16),
             pltpu.VMEM((QUARTERS, 16, full, WIDE), BF16),
             pltpu.VMEM((LINE, QUARTERS, 32, WIDE), BF16),
             pltpu.VMEM((SIDE, SIDE, LINE, items // devices, wide), BF16),
-            pltpu.VMEM((items, wide), BF16),
-            pltpu.VMEM((2, queries, WIDE), F32),
+            pltpu.VMEM((SIDE, SIDE, LINE * (items // devices), wide), BF16),
+            pltpu.VMEM((QUARTERS, queries, WIDE), F32),
             pltpu.VMEM((queries, wide), BF16),
             pltpu.VMEM((queries, items), BF16),
             pltpu.VMEM((queries, wide), BF16),

time: 135 us -> 130 us (0.963)
  Pallas kernels: 134 us -> 129 us
    pallas_call x1, Pallas kernels: 133 us -> 127 us  [on_device(): pl.pallas_call(functools.partial(step_kernel, scale), out_shape=(jax.Shap...]
where the time goes in v3:
time: 130 us; the launch traced here: 129 us
  Pallas kernels  129 us (99%)
    pallas_call x1, Pallas kernels, on_device(): pl.pallas_call(functools.partial(step_kernel, scale), out_shape=(jax.Shap...  127 us

profile of v3, /device:TPU:1, one launch (start us, length us, event | category | flops | bytes accessed | tf_op | source)
XLA Modules:
  0.0 129.5 jit_solution(16936349567302613940)
XLA Ops:
  0.6 127.2 %sampled_softmax_step.1 = (f32[28,1024]{1,0:T(8,128)}, f32[8,1024]{1,0:T(8,128)}, f32[8,128]{1,0:T(8,128)}) custom-call(bf16[1024,3584]{1,0:T(8,128)(2,1)} %hidden_ref.1, bf16[28,1024]{1,0:T(8,128)(2,1)} %w_ref.1, bf16[1024,1024]{1,0:T(8,128)(2,1)} %adapter_ref.1, bf16[16,1024]{1,0:T(8,128)(2,1)} %item_ref.1, s32[1,2048]{1,0:T(1,128)} %bitcast.4, ...), custom_call_target="tpu_custom_call" | custom-call | tf_op jit(solution)/shard_map/sampled_softmax_step/pallas_call | solution.py:555
  127.9 1.6 %finish.1 = (f32[28,1024]{1,0:T(8,128)}, f32[8,1024]{1,0:T(8,128)}, f32[1,1]{1,0:T(1,128)}) custom-call(f32[28,1024]{1,0:T(8,128)} %get-tuple-element.9.gw_in, f32[8,1024]{1,0:T(8,128)} %get-tuple-element.10.ga_in, f32[8,128]{1,0:T(8,128)} %get-tuple-element.11.loss_in), custom_call_target="tpu_custom_call" | custom-call | tf_op jit(solution)/shard_map/finish/pallas_call | solution.py:610

commit v4 on v3

--- a/solution.py
+++ b/solution.py
@@ -41,8 +41,10 @@
     scale, hidden_ref, w_ref, adapter_ref, item_ref, counts_ref, positive_ref, weight_ref,
     gw_ref, ga_ref, loss_ref,
     hid, hid_t, wall, xs, pool, adapted, partial, queries, coeff, grad_q, pulled, pos_col, weight_col, log_count,
-    sib_in, first_z, first_y, second_in, slot_out, slot_in, loss_out, loss_in,
-    load_sem, xs_s, xs_r, w_s, w_r, ws_s, ws_r, ez_s, ez_r, ey_s, ey_r, ex_s, ex_r, es_s, es_r, sib_s, sib_r, fz_s, fz_r, fy_s, fy_r, se_s, se_r,
+    sib_in, ga_sib, rz_in, lz_in, ry_in, ly_in, gx_in, gy_out, gy_in, gz_out, gz_in, g_out, g_in, shuffle,
+    second_in, slot_out, slot_in, loss_out, loss_in,
+    load_sem, xs_s, xs_r, w_s, w_r, ws_s, ws_r, ez_s, ez_r, ey_s, ey_r, ex_s, ex_r, es_s, es_r, sib_s, sib_r, gs_s, gs_r, rz_s, rz_r, lz_s, lz_r, ry_s, ry_r,
+    ly_s, ly_r, gx_s, gx_r, gy_s, gy_r, gz_s, gz_r, g_s, g_r, se_s, se_r,
     sl_s, sl_r, lo_s, lo_r,
 ):
     z, y, high, core, low = place()
@@ -376,61 +378,121 @@
         copy.wait_send()
     del sent[:-1]
 
-    full = wall.shape[2]
-    span = full - block_rows
-
-    def unit(k, q):
-        cols = columns(q)
-        upper = dot(hid_t[k], grad_q[:, cols])
-        lower = dot(pulled[...], queries[:, cols])
-        return jnp.reshape(upper, (SIDE, block_rows, WIDE)), jnp.reshape(lower, (SIDE, span, WIDE))
-
-    def sib_copy(p, k, c):
+    span = SIDE * LINE * adapter_rows
+    valid = pl.ds(0, block_rows)
+    first, second = 2 * core, 2 * core + 1
+
+    def sib_copy(p, k):
         four = pl.ds(k * SIDE, SIDE)
-        return remote(
-            wall.at[2 * c + p, four], sib_in.at[p, four], sib_s.at[p, k], sib_r.at[p, k], sibling
-        )
-
-    def fz_copy(o):
-        four = pl.ds(((z + o) % SIDE) * SIDE, SIDE)
-        return remote(wall.at[2 * core, four], first_z.at[o - 1], fz_s.at[o - 1], fz_r.at[o - 1], z_peer(o))
-
-    def fy_copy(k, o):
-        b = k * SIDE + (y + o) % SIDE
-        n = o - 1
-        return remote(wall.at[2 * core + 1, b], first_y.at[n, k], fy_s.at[n, k], fy_r.at[n, k], y_peer(o))
-
-    def reduce_group(i, carry):
-        k = (z + 1 + i) % SIDE
+        src = wall.at[2 * (1 - core) + p, four, valid]
+        return remote(src, sib_in.at[p, four], sib_s.at[p, k], sib_r.at[p, k], sibling)
+
+    def ga_sib_copy(p, k):
+        src = hid.at[SIDE * (2 * (1 - core) + p) + k, pl.ds(0, span)]
+        return remote(src, ga_sib.at[p, k], gs_s.at[p, k], gs_r.at[p, k], sibling)
+
+    def ring_z(o):
+        k = (z + 2) % SIDE
+        n = 0 if o == 1 else 1
+        src = wall.at[first, pl.ds(SIDE * k + 2 * n, 2), valid]
+        return remote(src, rz_in.at[n], rz_s.at[n], rz_r.at[n], z_peer(o))
+
+    def last_z(o, h):
+        k = (z + o) % SIDE
+        n = 0 if o == 1 else 1
+        src = wall.at[first, pl.ds(SIDE * k + 2 * h, 2), valid]
+        return remote(src, lz_in.at[n, pl.ds(2 * h, 2)], lz_s.at[n, h], lz_r.at[n, h], z_peer(o))
+
+    def ring_y(i, k):
+        b = SIDE * k + (y + 2) % SIDE
+        to = y_peer(1 if i < 2 else 3)
+        return remote(wall.at[second, b, valid], ry_in.at[i], ry_s.at[i], ry_r.at[i], to)
+
+    def last_y(i, k, o):
+        b = SIDE * k + (y + o) % SIDE
+        n = 0 if o == 1 else 1
+        return remote(wall.at[second, b, valid], ly_in.at[n, i], ly_s.at[n, i], ly_r.at[n, i], y_peer(o))
+
+    def gx_copy(k, p, o):
+        xx = (2 * high + low + o) % SIDE
+        rows = pl.ds(pl.multiple_of(xx * (span // SIDE), span // SIDE), span // SIDE)
+        src = hid.at[SIDE * (first + p) + k, rows]
+        return remote(src, gx_in.at[o - 1, p, k], gx_s.at[o - 1, p, k], gx_r.at[o - 1, p, k], x_peer(o))
+
+    row = lax.broadcasted_iota(jnp.int32, (span, span), 0)
+    col = lax.broadcasted_iota(jnp.int32, (span, span), 1)
+    from_row = ((row >> 4) & 3) * 64 + (row >> 7) * 32 + ((row >> 3) & 1) * 16 + ((row >> 6) & 1) * 8 + (row & 7)
+    shuffle[...] = jnp.where(col == from_row, 1.0, 0.0).astype(BF16)
+
+    hops = (2, 1, 3, 0)
+    for i, hop in enumerate(hops):
+        k = (z + hop) % SIDE
         four = pl.ds(k * SIDE, SIDE)
-        some = pool[:, :, :, :, pl.ds(pl.multiple_of(k * SIDE * span, SIDE * span), SIDE * span)]
-        pulled[...] = dot(coeff[...], jnp.reshape(some, (items_all, SIDE * span))).T.astype(BF16)
-        for p in range(2):
+
+        def weight_rows(q, k=k):
+            return jnp.reshape(dot(hid_t[k], grad_q[:, columns(q)]), (SIDE, block_rows, WIDE))
+
+        def for_sibling(p, carry, k=k, four=four):
             q = 2 * (1 - core) + p
-            upper, lower = unit(k, q)
-            wall[q, four, 0:block_rows, :] = upper.astype(BF16)
-            wall[q, four, block_rows:full, :] = lower.astype(BF16)
-            sib_copy(p, k, 1 - core).start()
-        for p in range(2):
+            wall[q, four, 0:block_rows, :] = weight_rows(q).astype(BF16)
+            sib_copy(p, k).start()
+            return carry
+
+        def for_self(p, carry, k=k, four=four):
             q = 2 * core + p
-            upper, lower = unit(k, q)
-            sib_copy(p, k, 1 - core).wait_recv()
-            wall[q, four, 0:block_rows, :] = (upper + sib_in[p, four, 0:block_rows, :].astype(F32)).astype(BF16)
-            wall[q, four, block_rows:full, :] = (lower + sib_in[p, four, block_rows:full, :].astype(F32)).astype(BF16)
-            if p == 0:
-                @pl.when(i < SIDE - 1)
-                def _():
-                    b = pl.ds(k * SIDE, SIDE)
-                    remote(
-                        wall.at[2 * core, b], first_z.at[i], fz_s.at[i], fz_r.at[i],
-                        device(k, y, high, core, low),
-                    ).start()
-            else:
-                for o in (1, 2, 3):
-                    fy_copy(k, o).start()
-        return carry
-
-    lax.fori_loop(0, SIDE, reduce_group, 0)
+            value = weight_rows(q)
+            sib_copy(p, k).wait_recv()
+            wall[q, four, 0:block_rows, :] = (value + sib_in[p, four].astype(F32)).astype(BF16)
+            return carry
+
+        lax.fori_loop(0, 2, for_sibling, 0)
+        lax.fori_loop(0, 2, for_self, 0)
+
+        if hop == 2:
+            ring_z(1).start()
+            ring_z(3).start()
+        elif hop:
+            last_z(hop, 1 if hop == 1 else 0).start()
+        ring_y(i, k).start()
+        last_y(i, k, 3 if i < 2 else 1).start()
+
+        some = pool[:, :, :, :, pl.ds(pl.multiple_of(k * span, span), span)]
+        pulled[...] = dot(coeff[...], jnp.reshape(some, (items_all, span))).T.astype(BF16)
+
+        if hop in (1, 3):
+            h = 0 if hop == 1 else 1
+            ring_z(hop).wait_recv()
+            for n in range(2):
+                b = SIDE * k + 2 * h + n
+                total_rows = wall[first, b, 0:block_rows, :].astype(F32) + rz_in[h, n].astype(F32)
+                wall[first, b, 0:block_rows, :] = total_rows.astype(BF16)
+            last_z(hop, h).start()
+
+        def adapter_sibling(p, carry, k=k):
+            q = 2 * (1 - core) + p
+            hid[SIDE * q + k, 0:span, :] = dot(pulled[...], queries[:, columns(q)]).astype(BF16)
+            ga_sib_copy(p, k).start()
+            return carry
+
+        def adapter_self(p, carry, k=k):
+            q = 2 * core + p
+            value = dot(pulled[...], queries[:, columns(q)])
+            ga_sib_copy(p, k).wait_recv()
+            value = (value + ga_sib[p, k].astype(F32)).astype(BF16)
+            hid[SIDE * q + k, 0:span, :] = dot(shuffle[...], value).astype(BF16)
+            for o in (1, 3, 2):
+                gx_copy(k, p, o).start()
+            return carry
+
+        lax.fori_loop(0, 2, adapter_sibling, 0)
+        lax.fori_loop(0, 2, adapter_self, 0)
+
+        o = 1 if i < 2 else 3
+        ring_y(i, k).wait_recv()
+        b = SIDE * k + (y + o) % SIDE
+        total_rows = wall[second, b, 0:block_rows, :].astype(F32) + ry_in[i].astype(F32)
+        wall[second, b, 0:block_rows, :] = total_rows.astype(BF16)
+        last_y(i, k, o).start()
 
     loss_out[1] = loss_sum(0, 1)
     for o in (1, 2, 3):
@@ -441,33 +503,31 @@
             b, to = z * SIDE + (y + o) % SIDE, y_peer(o)
         else:
             b, to = ((z + o) % SIDE) * SIDE + y, z_peer(o)
-        return remote(
-            wall.at[2 * core + p, b], second_in.at[p, o - 1], se_s.at[p, o - 1], se_r.at[p, o - 1], to
-        )
+        src = wall.at[2 * core + p, b, valid]
+        return remote(src, second_in.at[p, o - 1], se_s.at[p, o - 1], se_r.at[p, o - 1], to)
 
     mine = [None, None]
-    for o in (1, 2, 3):
-        fz_copy(o).wait_recv()
+    for o in (1, 3):
+        for h in range(2):
+            last_z(o, h).wait_recv()
     for o in (1, 2, 3, 0):
         yy = (y + o) % SIDE
-        value = wall[2 * core, z * SIDE + yy].astype(F32)
-        for n in range(3):
-            value = value + first_z[n, yy].astype(F32)
+        b = z * SIDE + yy
+        value = wall[first, b, 0:block_rows, :].astype(F32) + lz_in[0, yy].astype(F32) + lz_in[1, yy].astype(F32)
         if o:
-            wall[2 * core, z * SIDE + yy] = value.astype(BF16)
+            wall[first, b, 0:block_rows, :] = value.astype(BF16)
             second_copy(0, o).start()
         else:
             mine[0] = value
-    for o in (1, 2, 3, 0):
-        zz = (z + o) % SIDE
-        b = zz * SIDE + y
-        value = wall[2 * core + 1, b].astype(F32)
-        for n in range(3):
-            fy_copy(zz, n + 1).wait_recv()
-            value = value + first_y[n, zz].astype(F32)
-        if o:
-            wall[2 * core + 1, b] = value.astype(BF16)
-            second_copy(1, o).start()
+    for i, hop in enumerate(hops):
+        k = (z + hop) % SIDE
+        b = k * SIDE + y
+        last_y(i, k, 1).wait_recv()
+        last_y(i, k, 3).wait_recv()
+        value = wall[second, b, 0:block_rows, :].astype(F32) + ly_in[0, i].astype(F32) + ly_in[1, i].astype(F32)
+        if hop:
+            wall[second, b, 0:block_rows, :] = value.astype(BF16)
+            second_copy(1, hop).start()
         else:
             mine[1] = value
 
@@ -475,15 +535,33 @@
     for o in (1, 2, 3):
         loss_send(2, o - 1, y_peer(o))
 
+    def gy_copy(o):
+        return remote(gy_out.at[(y + o) % SIDE], gy_in.at[o - 1], gy_s.at[o - 1], gy_r.at[o - 1], y_peer(o))
+
+    def gz_copy(o):
+        return remote(gz_out.at[(z + o) % SIDE], gz_in.at[o - 1], gz_s.at[o - 1], gz_r.at[o - 1], z_peer(o))
+
+    pair = 2 * adapter_rows
+    quarter_rows = span // SIDE
+    here_x = pl.ds(pl.multiple_of((2 * high + low) * quarter_rows, quarter_rows), quarter_rows)
+    for k in range(SIDE):
+        for p in range(2):
+            value = hid[SIDE * (first + p) + k, here_x, :].astype(F32)
+            for o in (1, 2, 3):
+                gx_copy(k, p, o).wait_recv()
+                value = value + gx_in[o - 1, p, k].astype(F32)
+            value = value.astype(BF16)
+            for yy in range(SIDE):
+                gy_out[yy, p, k] = value[pair * yy:pair * (yy + 1)]
+    for o in (1, 2, 3):
+        gy_copy(o).start()
+
     tall = slot_out.shape[2]
-    shape = (LINE * tall, full)
+    shape = (LINE * tall, block_rows)
     row = lax.broadcasted_iota(jnp.int32, shape, 0)
     col = lax.broadcasted_iota(jnp.int32, shape, 1)
-    owner = sum(jnp.where(row >= tall * s, 1, 0) for s in range(1, LINE))
-    inner = row - tall * owner
-    from_w = (inner < own_rows) & (col == own_rows * owner + inner)
-    from_a = (inner >= 32) & (inner < 32 + adapter_rows) & (col == block_rows + adapter_rows * owner + inner - 32)
-    spread = jnp.where(from_w | from_a, 1.0, 0.0).astype(BF16)
+    owner, inner = row >> 5, row & 31
+    spread = jnp.where((inner < own_rows) & (col == own_rows * owner + inner), 1.0, 0.0).astype(BF16)
     for p in range(2):
         value = mine[p]
         for o in (1, 2, 3):
@@ -497,12 +575,33 @@
             slot_out.at[:, line_slot(k)], slot_in.at[k], sl_s.at[k], sl_r.at[k], line_peer(k)
         )
 
-    for k in (1, 4, 5, 3, 6, 7, 2):
+    for k in (4, 1, 5, 6, 3, 7, 2):
         slot_copy(k).start()
+
+    for o in (1, 2, 3):
+        gy_copy(o).wait_recv()
+    value = gy_out[y].astype(F32)
+    for o in (1, 2, 3):
+        value = value + gy_in[o - 1].astype(F32)
+    value = value.astype(BF16)
+    for k in range(SIDE):
+        gz_out[k] = value[:, k]
+    for o in (1, 2, 3):
+        gz_copy(o).start()
 
     loss_out[3] = loss_sum(2, 3)
     for n, k in enumerate((1, 4, 5)):
         loss_send(3, n, line_peer(k))
+
+    for o in (1, 2, 3):
+        gz_copy(o).wait_recv()
+    value = gz_out[z].astype(F32)
+    for o in (1, 2, 3):
+        value = value + gz_in[o - 1].astype(F32)
+    for c in range(2):
+        g_out[c] = value[:, c * adapter_rows:(c + 1) * adapter_rows]
+    g_copy = remote(g_out.at[1 - core], g_in, g_s, g_r, sibling)
+    g_copy.start()
 
     for k in range(1, LINE):
         slot_copy(k).wait_recv()
@@ -513,22 +612,36 @@
         other = slot_in[2, p].astype(F32)
         for k in (3, 6, 7):
             other = other + slot_in[k, p].astype(F32)
-        for value, c in ((same, core), (other, 1 - core)):
-            cols = pl.ds(pl.multiple_of((2 * c + p) * WIDE, WIDE), WIDE)
-            gw_ref[:, cols] = value[0:own_rows]
-            ga_ref[:, cols] = scale * value[32:32 + adapter_rows]
+        gw_ref[:, columns(2 * core + p)] = same[0:own_rows]
+        gw_ref[:, columns(2 * (1 - core) + p)] = other[0:own_rows]
+
+    g_copy.wait_recv()
+    for p in range(2):
+        ga_ref[:, columns(2 * core + p)] = scale * g_out[core, p]
+        ga_ref[:, columns(2 * (1 - core) + p)] = scale * g_in[p]
 
     loss_ref[...] = loss_sum(3, 3)
 
     for copy in sent:
         copy.wait_send()
-    for p in range(2):
-        for k in range(SIDE):
-            sib_copy(p, k, 1 - core).wait_send()
-    for o in (1, 2, 3):
-        fz_copy(o).wait_send()
-        for k in range(SIDE):
-            fy_copy(k, o).wait_send()
+    g_copy.wait_send()
+    for i, hop in enumerate(hops):
+        k = (z + hop) % SIDE
+        ring_y(i, k).wait_send()
+        for o in (1, 3):
+            last_y(i, k, o).wait_send()
+        for p in range(2):
+            sib_copy(p, k).wait_send()
+            ga_sib_copy(p, k).wait_send()
+            for o in (1, 2, 3):
+                gx_copy(k, p, o).wait_send()
+    for o in (1, 3):
+        ring_z(o).wait_send()
+        for h in range(2):
+            last_z(o, h).wait_send()
+    for o in (1, 2, 3):
+        gy_copy(o).wait_send()
+        gz_copy(o).wait_send()
         for p in range(2):
             second_copy(p, o).wait_send()
     for k in range(1, LINE):
@@ -548,7 +661,7 @@
     wide = adapter.shape[0]
     items = counts.shape[0]
     block = LINE * w_query.shape[0]
-    full = block + LINE * (wide // devices)
+    span = wide // SIDE
     sem = pltpu.SemaphoreType.DMA
     vmem = pl.BlockSpec(memory_space=pltpu.VMEM)
     anywhere = pl.BlockSpec(memory_space=pl.ANY)
@@ -564,7 +677,7 @@
         scratch_shapes=[
             pltpu.VMEM((16, queries, WIDE), BF16),
             pltpu.VMEM((SIDE, deep // SIDE, queries), BF16),
-            pltpu.VMEM((QUARTERS, 16, full, WIDE), BF16),
+            pltpu.VMEM((QUARTERS, 16, WIDE, WIDE), BF16),
             pltpu.VMEM((LINE, QUARTERS, 32, WIDE), BF16),
             pltpu.VMEM((SIDE, SIDE, LINE, items // devices, wide), BF16),
             pltpu.VMEM((SIDE, SIDE, LINE * (items // devices), wide), BF16),
@@ -576,12 +689,23 @@
             pltpu.VMEM((queries, 128), F32),
             pltpu.VMEM((queries, 128), F32),
             pltpu.VMEM((1, items), F32),
-            pltpu.VMEM((2, 16, full, WIDE), BF16),
-            pltpu.VMEM((3, SIDE, full, WIDE), BF16),
-            pltpu.VMEM((3, SIDE, full, WIDE), BF16),
-            pltpu.VMEM((2, 3, full, WIDE), BF16),
-            pltpu.VMEM((2, LINE, 48, WIDE), BF16),
-            pltpu.VMEM((LINE, 2, 48, WIDE), BF16),
+            pltpu.VMEM((2, 16, block, WIDE), BF16),
+            pltpu.VMEM((2, SIDE, span, WIDE), BF16),
+            pltpu.VMEM((2, 2, block, WIDE), BF16),
+            pltpu.VMEM((2, SIDE, block, WIDE), BF16),
+            pltpu.VMEM((SIDE, block, WIDE), BF16),
+            pltpu.VMEM((2, SIDE, block, WIDE), BF16),
+            pltpu.VMEM((3, 2, SIDE, span // SIDE, WIDE), BF16),
+            pltpu.VMEM((SIDE, 2, SIDE, span // 16, WIDE), BF16),
+            pltpu.VMEM((3, 2, SIDE, span // 16, WIDE), BF16),
+            pltpu.VMEM((SIDE, 2, span // 16, WIDE), BF16),
+            pltpu.VMEM((3, 2, span // 16, WIDE), BF16),
+            pltpu.VMEM((2, 2, wide // devices, WIDE), F32),
+            pltpu.VMEM((2, wide // devices, WIDE), F32),
+            pltpu.VMEM((span, span), BF16),
+            pltpu.VMEM((2, 3, block, WIDE), BF16),
+            pltpu.VMEM((2, LINE, 32, WIDE), BF16),
+            pltpu.VMEM((LINE, 2, 32, WIDE), BF16),
             pltpu.VMEM((4, 8, 128), F32),
             pltpu.VMEM((4, 3, 8, 128), F32),
             sem((SIDE + 1,)),
@@ -593,8 +717,15 @@
             sem((3, SIDE)), sem((3, SIDE)),
             sem((SIDE, SIDE)), sem((SIDE, SIDE)),
             sem((2, SIDE)), sem((2, SIDE)),
+            sem((2, SIDE)), sem((2, SIDE)),
+            sem((2,)), sem((2,)),
+            sem((2, 2)), sem((2, 2)),
+            sem((SIDE,)), sem((SIDE,)),
+            sem((2, SIDE)), sem((2, SIDE)),
+            sem((3, 2, SIDE)), sem((3, 2, SIDE)),
             sem((3,)), sem((3,)),
-            sem((3, SIDE)), sem((3, SIDE)),
+            sem((3,)), sem((3,)),
+            sem, sem,
             sem((2, 3)), sem((2, 3)),
             sem((LINE,)), sem((LINE,)),
             sem((4, 3)), sem((4, 3)),

time: 130 us -> 123 us (0.946)
  Pallas kernels: 129 us -> 123 us
    pallas_call x1, Pallas kernels: 127 us -> 121 us  [on_device(): pl.pallas_call(functools.partial(step_kernel, scale), out_shape=(jax.Shap...]
where the time goes in v4:
time: 123 us
  Pallas kernels  123 us (100%)
    pallas_call x1, Pallas kernels, on_device(): pl.pallas_call(functools.partial(step_kernel, scale), out_shape=(jax.Shap...  121 us

profile of v4, /device:TPU:1, one launch (start us, length us, event | category | flops | bytes accessed | tf_op | source)
XLA Modules:
  0.0 123.3 jit_solution(2551683081483387843)
XLA Ops:
  0.6 121.1 %sampled_softmax_step.1 = (f32[28,1024]{1,0:T(8,128)}, f32[8,1024]{1,0:T(8,128)}, f32[8,128]{1,0:T(8,128)}) custom-call(bf16[1024,3584]{1,0:T(8,128)(2,1)} %hidden_ref.1, bf16[28,1024]{1,0:T(8,128)(2,1)} %w_ref.1, bf16[1024,1024]{1,0:T(8,128)(2,1)} %adapter_ref.1, bf16[16,1024]{1,0:T(8,128)(2,1)} %item_ref.1, s32[1,2048]{1,0:T(1,128)} %bitcast.4, ...), custom_call_target="tpu_custom_call" | custom-call | tf_op jit(solution)/shard_map/sampled_softmax_step/pallas_call | solution.py:668
  121.7 1.6 %finish.1 = (f32[28,1024]{1,0:T(8,128)}, f32[8,1024]{1,0:T(8,128)}, f32[1,1]{1,0:T(1,128)}) custom-call(f32[28,1024]{1,0:T(8,128)} %get-tuple-element.9.gw_in, f32[8,1024]{1,0:T(8,128)} %get-tuple-element.10.ga_in, f32[8,128]{1,0:T(8,128)} %get-tuple-element.11.loss_in), custom_call_target="tpu_custom_call" | custom-call | tf_op jit(solution)/shard_map/finish/pallas_call | solution.py:741
